TPU v7x, 128 devices: a whole 4x4x4 slice. The times are simulated.
128 devices in a mesh: tensor: 16 (over z_lo, y, core), dp: 8 (over z_hi, x).
Axes of the slice: x: 4, y: 4, z: 4 (z_hi: 2, z_lo: 2; z = z_hi * 2 + z_lo), core: 2. Of those that a mesh axis runs over, the one named last changes fastest.
Arguments:
- inputs: bfloat16 [8, 640, 4096], P('dp', 'tensor'), may hold values from -6 to 6
- out_grad: bfloat16 [8, 640, 4096], P('dp', 'tensor'), may hold values from -6 to 6
- w_gate: bfloat16 [4096, 14336], P(None, 'tensor'), may hold values from -0.09375 to 0.09375
- w_up: bfloat16 [4096, 14336], P(None, 'tensor'), may hold values from -0.09375 to 0.09375
- w_down: bfloat16 [14336, 4096], P('tensor'), may hold values from -0.046875 to 0.046875
Outputs:
- input_grad: bfloat16 [8, 640, 4096], P('dp', 'tensor')
- grad_gate: bfloat16 [4096, 14336], P('dp', 'tensor')
- grad_up: bfloat16 [4096, 14336], P('dp', 'tensor')
- grad_down: bfloat16 [14336, 4096], P('tensor', 'dp')
All inputs are finite; a program needn't handle non-finite values.
Results may differ from a plain program's by a relative error of at most 0.023.
Values may be sent and summed in bfloat16 or wider, within the bound.
A program may use at most 192 MiB of HBM per device.

v0:
```python
import math

import jax
import jax.numpy as jnp
from jax import lax
from jax.sharding import PartitionSpec as P


def contract_rows(left, right):
    return lax.dot_general(
        left, right, (((0,), (0,)), ((), ())), preferred_element_type=jnp.float32
    )


def contract_cols(left, right):
    return lax.dot_general(
        left, right, (((1,), (1,)), ((), ())), preferred_element_type=jnp.float32
    )


def local(inputs, out_grad, w_gate, w_up, w_down):
    slab_in_all, slab_grad_all = (
        lax.all_gather(inputs, "tensor", axis=1, tiled=True),
        lax.all_gather(out_grad, "tensor", axis=1, tiled=True),
    )
    slab_in = slab_in_all[0]
    slab_grad = slab_grad_all[0]
    slab_len = slab_in.shape[0]
    gate = jnp.dot(slab_in, w_gate, preferred_element_type=jnp.float32)
    up = jnp.dot(slab_in, w_up, preferred_element_type=jnp.float32)
    sigmoid_gate = jax.nn.sigmoid(gate)
    hidden = (gate * sigmoid_gate * up).astype(jnp.bfloat16)
    hidden_grad = contract_cols(slab_grad, w_down)
    gate_grad = (hidden_grad * up * sigmoid_gate * (1.0 + gate * (1.0 - sigmoid_gate))).astype(
        jnp.bfloat16
    )
    up_grad = (hidden_grad * gate * sigmoid_gate).astype(jnp.bfloat16)
    back = lax.psum_scatter(
        (contract_cols(gate_grad, w_gate) + contract_cols(up_grad, w_up)).astype(jnp.bfloat16),
        "tensor",
        scatter_dimension=0,
        tiled=True,
    )
    input_grad = back[None]
    groups = lax.axis_size("dp")
    scale_factor = 1.0 / math.sqrt(slab_len * groups)
    part_gate = contract_rows(slab_in, gate_grad)
    part_up = contract_rows(slab_in, up_grad)
    part_down = contract_rows(hidden, slab_grad)
    sum_gate, sum_up = (
        lax.psum_scatter(
            part_gate.astype(jnp.bfloat16), "dp", scatter_dimension=0, tiled=True
        ).astype(jnp.float32),
        lax.psum_scatter(
            part_up.astype(jnp.bfloat16), "dp", scatter_dimension=0, tiled=True
        ).astype(jnp.float32),
    )
    sum_down = lax.psum_scatter(
        part_down.astype(jnp.bfloat16), "dp", scatter_dimension=1, tiled=True
    ).astype(jnp.float32)
    grad_gate = (sum_gate * scale_factor).astype(jnp.bfloat16)
    grad_up = (sum_up * scale_factor).astype(jnp.bfloat16)
    grad_down = (sum_down * scale_factor).astype(jnp.bfloat16)
    return (input_grad, grad_gate, grad_up, grad_down)


def solution(mesh):
    placed = (
        P("dp", "tensor", None),
        P("dp", "tensor", None),
        P(None, "tensor"),
        P(None, "tensor"),
        P("tensor", None),
    )
    return jax.shard_map(
        local,
        mesh=mesh,
        in_specs=placed,
        out_specs=(
            P("dp", "tensor", None),
            P("dp", "tensor"),
            P("dp", "tensor"),
            P("tensor", "dp"),
        ),
        check_vma=False,
    )
```

profile of v0, /device:TPU:64, one launch (start us, length us, event | category | flops | bytes accessed | tf_op | source)
XLA Modules:
  0.0 515.2 jit_solution(16533253198936883663)
XLA Ops:
  7.2 0.0 all-gather.5.cloned.1.call-start
  7.2 0.7 all-gather.5.cloned.1.call-update
  7.9 0.0 all-gather.3.cloned.1.call-start
  7.9 0.7 all-gather.3.cloned.1.call-update
  8.6 0.0 reduce-scatter.9.cloned.1.call-start
  8.7 41.8 %all-gather.5.cloned.1.call-done = bf16[1,640,4096]{2,1,0:T(8,128)(2,1)} async-done(((bf16[1,40,4096]{2,1,0:T(8,128)(2,1)}), bf16[1,640,4096]{2,1,0:T(8,128)(2,1)}) %all-gather.5.cloned.1.call-update) | async-done | bytes 5242896 | tf_op jit(solution)/shard_map/all_gather | solution.py:23
  50.5 0.0 copy-start
  50.5 12.3 %fusion.2 = f32[640,896]{1,0:T(8,128)S(1)} fusion(bf16[4096,896]{1,0:T(8,128)(2,1)} %param.7, bf16[1,640,4096]{2,1,0:T(8,128)(2,1)} %all-gather.5.cloned.1.call-done), kind=kOutput, calls=%fused_computation.6 | convolution fusion | flops 4697620480 | bytes 14876672 | tf_op jit(solution)/shard_map/dot_general | solution.py:29
  62.8 0.0 copy-done
  62.8 9.2 %fusion.4 = f32[640,896]{1,0:T(8,128)} fusion(bf16[4096,896]{1,0:T(8,128)(2,1)} %param.8, bf16[1,640,4096]{2,1,0:T(8,128)(2,1)S(1)} %copy-done), kind=kOutput, calls=%fused_computation.8 | convolution fusion | flops 4697620480 | bytes 14876672 | tf_op jit(solution)/shard_map/dot_general | solution.py:30
  72.0 19.8 %all-gather.3.cloned.1.call-done = bf16[1,640,4096]{2,1,0:T(8,128)(2,1)} async-done(((bf16[1,40,4096]{2,1,0:T(8,128)(2,1)}), bf16[1,640,4096]{2,1,0:T(8,128)(2,1)}) %all-gather.3.cloned.1.call-update) | async-done | bytes 5242896 | tf_op jit(solution)/shard_map/all_gather | solution.py:24
  91.7 0.0 copy-start.1
  91.7 11.5 %multiply_convert_fusion.1 = (bf16[640,896]{1,0:T(8,128)(2,1)S(1)}, bf16[640,896]{1,0:T(8,128)(2,1)}) fusion(f32[640,896]{1,0:T(8,128)S(1)} %fusion.2, f32[640,896]{1,0:T(8,128)} %fusion.4, bf16[896,4096]{1,0:T(8,128)(2,1)} %param.9, bf16[1,640,4096]{2,1,0:T(8,128)(2,1)} %all-gather.3.cloned.1.call-done), kind=kOutput, calls=%fused_computation.14 | convolution fusion | flops 4705075200 | bytes 19464192 | tf_op jit(solution)/shard_map/dot_general | solution.py:16
  103.2 0.0 copy-done.1
  103.2 8.1 %convert_bitcast_fusion = bf16[4096,896]{0,1:T(8,128)(2,1)} fusion(bf16[640,896]{1,0:T(8,128)(2,1)S(1)} %get-tuple-element.8, bf16[1,640,4096]{2,1,0:T(8,128)(2,1)S(1)} %copy-done.1), kind=kOutput, calls=%fused_computation.1 | convolution fusion | flops 4701290496 | bytes 13729792 | tf_op jit(solution)/shard_map/dot_general | solution.py:10
  111.3 0.0 reduce-scatter.9.cloned.1.call-update
  111.4 0.2 reduce-scatter.7.cloned.1.call-start
  111.6 10.1 %convert_bitcast_fusion.1 = bf16[4096,896]{0,1:T(8,128)(2,1)} fusion(bf16[640,896]{1,0:T(8,128)(2,1)} %get-tuple-element.9, bf16[1,640,4096]{2,1,0:T(8,128)(2,1)} %all-gather.5.cloned.1.call-done), kind=kOutput, calls=%fused_computation.2 | convolution fusion | flops 4701290496 | bytes 13729792 | tf_op jit(solution)/shard_map/dot_general | solution.py:10
  121.7 0.0 reduce-scatter.7.cloned.1.call-update
  121.7 0.0 reduce-scatter.11.cloned.1.call-start
  121.8 10.6 %convolution_convert_fusion = bf16[896,4096]{1,0:T(8,128)(2,1)} fusion(bf16[1,640,4096]{2,1,0:T(8,128)(2,1)} %all-gather.3.cloned.1.call-done, f32[640,896]{1,0:T(8,128)} %fusion.4, f32[640,896]{1,0:T(8,128)S(1)} %fusion.2), kind=kOutput, calls=%fused_computation.3 | convolution fusion | flops 4704731136 | bytes 17170432 | tf_op jit(solution)/shard_map/dot_general | solution.py:10
  132.3 0.0 copy-start.2
  132.3 0.0 reduce-scatter.11.cloned.1.call-update
  132.4 0.0 reduce-scatter.5.cloned.1.call-start
  132.4 1.2 copy-done.2
  133.6 8.0 %fusion.11 = f32[640,4096]{1,0:T(8,128)S(1)} fusion(bf16[640,896]{1,0:T(8,128)(2,1)S(1)} %copy-done.2, bf16[4096,896]{1,0:T(8,128)(2,1)} %param.7), kind=kOutput, calls=%fused_computation.22 | convolution fusion | flops 4697620480 | bytes 18972672 | tf_op jit(solution)/shard_map/dot_general | solution.py:16
  141.6 11.1 %add_convert_fusion = bf16[640,4096]{1,0:T(8,128)(2,1)} fusion(f32[640,4096]{1,0:T(8,128)S(1)} %fusion.11, bf16[640,896]{1,0:T(8,128)(2,1)S(1)} %get-tuple-element.8, bf16[4096,896]{1,0:T(8,128)(2,1)} %param.8), kind=kOutput, calls=%fused_computation | convolution fusion | flops 4702863360 | bytes 24215552 | tf_op jit(solution)/shard_map/dot_general | solution.py:16
  152.7 0.0 reduce-scatter.5.cloned.1.call-update
  152.7 64.1 %reduce-scatter.9.cloned.1.call-done = bf16[512,896]{0,1:T(8,128)(2,1)} async-done(((bf16[4096,896]{0,1:T(8,128)(2,1)}), bf16[512,896]{0,1:T(8,128)(2,1)}) %reduce-scatter.9.cloned.1.call-update) | async-done | bytes 917520 | tf_op jit(solution)/shard_map/reduce_scatter | solution.py:54
  216.8 1.3 multiply_convert_fusion.4
  218.2 1.3 copy.10
  219.4 107.2 %reduce-scatter.7.cloned.1.call-done = bf16[512,896]{0,1:T(8,128)(2,1)} async-done(((bf16[4096,896]{0,1:T(8,128)(2,1)}), bf16[512,896]{0,1:T(8,128)(2,1)}) %reduce-scatter.7.cloned.1.call-update) | async-done | bytes 917520 | tf_op jit(solution)/shard_map/reduce_scatter | solution.py:51
  326.6 1.3 multiply_convert_fusion.5
  327.9 1.3 copy.9
  329.2 107.1 %reduce-scatter.11.cloned.1.call-done = bf16[896,512]{1,0:T(8,128)(2,1)} async-done(((bf16[896,4096]{1,0:T(8,128)(2,1)}), bf16[896,512]{1,0:T(8,128)(2,1)}) %reduce-scatter.11.cloned.1.call-update) | async-done | bytes 917520 | tf_op jit(solution)/shard_map/reduce_scatter | solution.py:58
  436.3 2.3 multiply_convert_fusion.3
  438.6 69.8 %reduce-scatter.5.cloned.1.call-done = bf16[40,4096]{1,0:T(8,128)(2,1)} async-done(((bf16[640,4096]{1,0:T(8,128)(2,1)}), bf16[40,4096]{1,0:T(8,128)(2,1)}) %reduce-scatter.5.cloned.1.call-update) | async-done | bytes 327696 | tf_op jit(solution)/shard_map/reduce_scatter | solution.py:38
Async XLA Ops:
  7.2 43.3 %all-gather.5.cloned.1.call-start = ((), (), s32[]{:S(2)}) async-start(), calls=%async_computation.5 | async-start | bytes 5570560 | tf_op jit(solution)/shard_map/all_gather | solution.py:23
  7.9 83.8 %all-gather.3.cloned.1.call-start = ((), (), s32[]{:S(2)}) async-start(), calls=%async_computation.4 | async-start | bytes 5570560 | tf_op jit(solution)/shard_map/all_gather | solution.py:24
  8.6 208.2 %reduce-scatter.9.cloned.1.call-start = ((), (), s32[]{:S(2)}) async-start(), calls=%async_computation.8 | async-start | bytes 8257536 | tf_op jit(solution)/shard_map/reduce_scatter | solution.py:54
  50.5 12.3 %copy-start = (bf16[1,640,4096]{2,1,0:T(8,128)(2,1)S(1)}, bf16[1,640,4096]{2,1,0:T(8,128)(2,1)}, u32[]{:S(2)}) copy-start(bf16[1,640,4096]{2,1,0:T(8,128)(2,1)} %all-gather.5.cloned.1.call-done) | copy-start | bytes 15728644
  91.7 11.5 %copy-start.1 = (bf16[1,640,4096]{2,1,0:T(8,128)(2,1)S(1)}, bf16[1,640,4096]{2,1,0:T(8,128)(2,1)}, u32[]{:S(2)}) copy-start(bf16[1,640,4096]{2,1,0:T(8,128)(2,1)} %all-gather.5.cloned.1.call-done) | copy-start | bytes 15728644
  111.4 215.2 %reduce-scatter.7.cloned.1.call-start = ((), (), s32[]{:S(2)}) async-start(), calls=%async_computation.7 | async-start | bytes 8257536 | tf_op jit(solution)/shard_map/reduce_scatter | solution.py:51
  121.7 314.6 %reduce-scatter.11.cloned.1.call-start = ((), (), s32[]{:S(2)}) async-start(), calls=%async_computation.9 | async-start | bytes 8257536 | tf_op jit(solution)/shard_map/reduce_scatter | solution.py:58
  132.3 1.3 copy-start.2
  132.4 376.0 %reduce-scatter.5.cloned.1.call-start = ((), (), s32[]{:S(2)}) async-start(), calls=%async_computation.6 | async-start | bytes 5570560 | tf_op jit(solution)/shard_map/reduce_scatter | solution.py:38
Sparse Core Ops, SparseCore 0:
  9.7 40.7 all-gather.4
  52.2 39.4 all-gather.2
  111.5 105.2 reduce-scatter.8
  221.1 105.4 reduce-scatter.6
  330.4 105.9 reduce-scatter.10
  439.3 69.0 reduce-scatter.4
where the time goes:
time: 517 us; the launch traced here: 515 us
  waiting for transfers between devices  411 us (79%)
  matrix products  80.8 us (16%)
  between operations  14.1 us (3%)
    reduce_scatter x1, waiting for transfers between devices, local(): lax.psum_scatter(part_gate.astype(jnp.bfloat16), 'dp', scatter_dimension=...  107 us
    reduce_scatter x1, waiting for transfers between devices, local(): lax.psum_scatter(part_down.astype(jnp.bfloat16), 'dp', scatter_dimension=...  107 us
    reduce_scatter x1, waiting for transfers between devices, local(): lax.psum_scatter((contract_cols(gate_grad, w_gate) + contract_cols(up_gra...  69.8 us
    reduce_scatter x1, waiting for transfers between devices, local(): lax.psum_scatter(part_up.astype(jnp.bfloat16), 'dp', scatter_dimension=0,...  64.1 us
    all_gather x1, waiting for transfers between devices, local(): lax.all_gather(inputs, 'tensor', axis=1, tiled=True)  41.8 us
    dot_general x3, matrix products, contract_cols(): lax.dot_general(left, right, (((1,), (1,)), ((), ())), preferred_element_...  30.5 us
    dot_general x3, matrix products, contract_rows(): lax.dot_general(left, right, (((0,), (0,)), ((), ())), preferred_element_...  28.8 us
    all_gather x1, waiting for transfers between devices, local(): lax.all_gather(out_grad, 'tensor', axis=1, tiled=True)  19.8 us
  transfers between devices with their start and end apart: 6, of which 6 were waited for; matrix products, arithmetic and copies ran while one was open for 13% of the time, Pallas kernels for 0%

commit v1 on v0

v1 whole, which is shorter than its diff:
```python
import functools
import math

import jax
import jax.numpy as jnp
from jax import lax
from jax.experimental import pallas as pl
from jax.experimental.pallas import tpu as pltpu
from jax.sharding import PartitionSpec as P

BF16 = jnp.bfloat16
F32 = jnp.float32
NX = NY = NZ = 4
NT = (((1,), (1,)), ((), ()))
HIDDEN, GATE, UP = 0, 1, 2
JOBS = ((HIDDEN, True), (HIDDEN, False), (GATE, True), (UP, True), (GATE, False), (UP, False))


def nt(left, right):
    return lax.dot_general(left, right, NT, preferred_element_type=F32)


def kernel(
    scale, x_in, g_in, wg_hbm, wu_hbm, wd_hbm,
    out_g, out_u, out_d, ig_main, ig_tail, p_hbm, s_hbm, r_hbm,
    xg, wg, wu, wd, fa, fb, lt, gu, own, fwd, got, pst, tail, ptail, fin, fin2,
    w_sem, core_ss, core_rs, ag_ss, ag_rs, sh_ss, sh_rs, x_ss, x_rs,
    p_ss, p_rs, r_ss, r_rs, z_ss, z_rs, o_ss, o_rs, loc_sem, fetch_sem,
):
    rows, width = x_in.shape
    half = width // 2
    quarter = half // 2
    main = rows // 16 * 16
    rest = rows - main
    chip = 2 * rows
    tokens = xg.shape[1]
    plane = NZ * chip
    hid = lt.shape[1]
    pad = wg.shape[1]
    full = pad - 128
    block = width // 8

    t = lax.axis_index("tensor")
    d = lax.axis_index("dp")
    c = lax.rem(t, 2)
    y = lax.rem(t // 2, NY)
    zl = t // (2 * NY)
    x = lax.rem(d, NX)
    zh = d // NX
    z = 2 * zh + zl

    def dev(dx, yy, zz, cc):
        xx = lax.rem(x + dx + NX, NX)
        return {"tensor": (lax.rem(zz, 2) * NY + yy) * 2 + cc, "dp": (zz // 2) * NX + xx}

    def ring(v, off):
        return lax.rem(v + off + 4, 4)

    def frame(cc):
        return y + cc * (z - y), z + cc * (y - z)

    def slot(cc, uu, vv):
        yy, zz = uu + cc * (vv - uu), vv + cc * (uu - vv)
        return NZ * yy + zz

    def uv_dev(uu, vv):
        return dev(0, uu + c * (vv - uu), vv + c * (uu - vv), c)

    def at_rows(index, count=chip, offset=0):
        return pl.ds(pl.multiple_of(chip * index + offset, 16), count)

    partner = dev(0, y, z, 1 - c)
    right, left = dev(1, y, z, c), dev(-1, y, z, c)
    across = dev(0, y, ring(z, 2), c)
    pending = []

    def rcopy(src, dst, ss, rs, to):
        return pltpu.make_async_remote_copy(
            src_ref=src, dst_ref=dst, send_sem=ss, recv_sem=rs,
            device_id=to, device_id_type=pl.DeviceIdType.MESH,
        )

    def send(src, dst, ss, rs, to):
        copy = rcopy(src, dst, ss, rs, to)
        copy.start()
        pending.append(copy)
        return copy

    first = pl.ds(pl.multiple_of(zh * full, 128), full)
    shared = pl.ds(2 * full, pad - full)
    loads = [
        pltpu.make_async_copy(wg_hbm.at[:, first], wg.at[:, pl.ds(0, full)], w_sem.at[0]),
        pltpu.make_async_copy(wg_hbm.at[:, shared], wg.at[:, pl.ds(full, pad - full)], w_sem.at[1]),
        pltpu.make_async_copy(wu_hbm.at[:, first], wu.at[:, pl.ds(0, full)], w_sem.at[2]),
        pltpu.make_async_copy(wu_hbm.at[:, shared], wu.at[:, pl.ds(full, pad - full)], w_sem.at[3]),
        pltpu.make_async_copy(wd_hbm.at[first, :], wd.at[pl.ds(0, full), :], w_sem.at[4]),
        pltpu.make_async_copy(wd_hbm.at[shared, :], wd.at[pl.ds(full, pad - full), :], w_sem.at[5]),
    ]
    for load in loads:
        load.start()

    barrier = pltpu.get_barrier_semaphore()
    greeted = [partner, right, left]
    for ry in range(NY):
        for rz in range(NZ):
            if ry or rz:
                greeted.append(dev(0, ring(y, ry), ring(z, rz), c))
    for to in greeted:
        pl.semaphore_signal(barrier, inc=1, device_id=to, device_id_type=pl.DeviceIdType.MESH)

    me = NZ * y + z
    for a, src in enumerate((x_in, g_in)):
        xg[a, at_rows(me, main, main * c), :] = src[0:main, :]
        last = src[main:rows, :].astype(F32)
        none = jnp.zeros_like(last)
        tail[a] = jnp.concatenate(
            [jnp.where(c == 0, last, none), jnp.where(c == 0, none, last)], axis=0
        ).astype(BF16)
    pl.semaphore_wait(barrier, len(greeted))

    for a in range(2):
        mine = xg.at[a, at_rows(me, main, main * c), :]
        send(mine, mine, core_ss.at[a, 0], core_rs.at[a, 0], partner)
        send(tail.at[a], ptail.at[a], core_ss.at[a, 1], core_rs.at[a, 1], partner)

    u, v = frame(c)
    pu, pv = frame(1 - c)
    GROUPS = (0, -1, 1, 2)

    def region(a, ou, ov, part=None):
        col = c * half if part is None else c * half + part * quarter
        return xg.at[
            a, at_rows(slot(c, ring(u, ou), ring(v, ov))),
            pl.ds(pl.multiple_of(col, quarter), half if part is None else quarter),
        ]

    def partner_region(a, ou, ov):
        return xg.at[
            a, at_rows(slot(1 - c, ring(pu, ou), ring(pv, ov))),
            pl.ds(pl.multiple_of((1 - c) * half, quarter), half),
        ]

    def place(label):
        if label < 4:
            base, kind, axis = 0, label, 0
        else:
            base, kind, axis = GROUPS[(label - 4) // 4], label % 4, 1
        off = (-1, 1, 2, 2)[kind]
        part = (None, None, 0, 1)[kind]
        return (off, 0, part) if axis == 0 else (base, off, part)

    def arrived(a, label):
        where = region(a, *place(label))
        rcopy(where, where, ag_ss.at[a, label], ag_rs.at[a, label], partner).wait_recv()

    def pass_on(a, label, where, to):
        send(where, where, ag_ss.at[a, label], ag_rs.at[a, label], to)

    u_plus, u_minus = uv_dev(ring(u, 1), v), uv_dev(ring(u, -1), v)
    v_plus, v_minus = uv_dev(u, ring(v, 1)), uv_dev(u, ring(v, -1))

    def share(a, ou, ov):
        n = 4 * (ou % 4) + ov % 4
        where = region(a, ou, ov)
        send(where, where, sh_ss.at[a, n], sh_rs.at[a, n], partner)

    def along_v(a, r):
        where = region(a, GROUPS[r], 0)
        pass_on(a, 4 + 4 * r, where, v_plus)
        pass_on(a, 5 + 4 * r, where, v_minus)

    def gather_steps(a):
        def begin():
            mine = xg.at[a, at_rows(me, main, main * (1 - c)), :]
            rcopy(mine, mine, core_ss.at[a, 0], core_rs.at[a, 0], partner).wait_recv()
            rcopy(tail.at[a], ptail.at[a], core_ss.at[a, 1], core_rs.at[a, 1], partner).wait_recv()
            xg[a, at_rows(me, 2 * rest, 2 * main), :] = tail[a] + ptail[a]
            where = region(a, 0, 0)
            pass_on(a, 0, where, u_plus)
            pass_on(a, 1, where, u_minus)
            along_v(a, 0)

        def u_step(kind):
            off = (-1, 1)[kind]
            arrived(a, kind)
            pass_on(a, 2 + kind, region(a, off, 0, kind), (u_plus, u_minus)[kind])
            along_v(a, 1 + kind)
            share(a, off, 0)

        def u_last():
            arrived(a, 2)
            arrived(a, 3)
            along_v(a, 3)
            share(a, 2, 0)

        def v_step(r, kind):
            off = (-1, 1)[kind]
            arrived(a, 4 + 4 * r + kind)
            pass_on(a, 6 + 4 * r + kind, region(a, GROUPS[r], off, kind), (v_plus, v_minus)[kind])
            share(a, GROUPS[r], off)

        def v_last(r):
            arrived(a, 6 + 4 * r)
            arrived(a, 7 + 4 * r)
            share(a, GROUPS[r], 2)

        def take():
            for ou in range(4):
                for ov in range(4):
                    if ou or ov:
                        n = 4 * ou + ov
                        where = partner_region(a, ou, ov)
                        rcopy(where, where, sh_ss.at[a, n], sh_rs.at[a, n], partner).wait_recv()

        steps = [begin, functools.partial(u_step, 0), functools.partial(u_step, 1), u_last]
        for r in range(4):
            steps += [functools.partial(v_step, r, 0), functools.partial(v_step, r, 1)]
            if r:
                steps.append(functools.partial(v_last, r - 1))
        steps += [functools.partial(v_last, 3), take]
        return steps

    steps_x, steps_g = gather_steps(0), gather_steps(1)
    steps_x[0]()
    steps_g[0]()
    for step in steps_x[1:4]:
        step()
    for step in steps_g[1:4]:
        step()
    for step in steps_x[4:]:
        step()
    later = steps_g[4:]

    for load in loads[:4]:
        load.wait()
    piece = 256

    def put_transposed(which, n, span, value):
        turned = value.T
        if n == 0:
            lt[which, 0:piece, span] = turned
        else:
            keep = full - piece
            lt[which, piece:full, span] = turned[0:keep]
            side = hid - full
            lt[which, full:hid, span] = jnp.where(
                zh == 0, turned[keep:keep + side], turned[keep + side:keep + 2 * side]
            )

    def gate_piece(i):
        span = pl.ds(pl.multiple_of(i * piece, piece), piece)
        slab = xg[0, span, :]
        for n in range(2):
            cols = pl.ds(n * piece, piece)
            gate = jnp.dot(slab, wg[:, cols], preferred_element_type=F32)
            up = jnp.dot(slab, wu[:, cols], preferred_element_type=F32)
            sig = jax.nn.sigmoid(gate)
            act = gate * sig
            fb[span, cols] = act.astype(BF16)
            fa[span, cols] = (up * sig * (1.0 + gate * (1.0 - sig))).astype(BF16)
            put_transposed(HIDDEN, n, span, (act * up).astype(BF16))

    pieces = tokens // piece
    done = 0
    for i in range(pieces):
        gate_piece(i)
        until = len(later) * (i + 1) // pieces
        for step in later[done:until]:
            step()
        done = until

    def factors(j, xx):
        which, other = JOBS[j]
        side = 1 - zh if other else zh
        col = pl.multiple_of(side * half + lax.rem(xx, NX) * block, block)
        return jnp.dot(
            lt[which], xg[1 if which == HIDDEN else 0, :, pl.ds(col, block)],
            preferred_element_type=F32,
        )

    top, low = pl.ds(0, hid // 2), pl.ds(hid // 2, hid // 2)
    R, OPP, L = 0, 1, 2
    opposite = {}

    def multiply(j):
        def one(s, carry):
            own[j, s] = factors(j, x + 1 + s).astype(BF16)
            return carry

        lax.fori_loop(0, 3, one, 0)
        opposite[j] = [
            rcopy(own.at[j, OPP, top], fwd.at[j, 0], x_ss.at[j, 0], x_rs.at[j, 0], right),
            rcopy(own.at[j, OPP, low], fwd.at[j, 1], x_ss.at[j, 1], x_rs.at[j, 1], left),
        ]
        for copy in opposite[j]:
            copy.start()
        send(own.at[j, R, low], got.at[j, 0, low], x_ss.at[j, 2], x_rs.at[j, 2], right)
        send(own.at[j, L, top], got.at[j, 1, top], x_ss.at[j, 3], x_rs.at[j, 3], left)

    def add_on(j):
        for n, (s, part, to) in enumerate(((R, top, right), (L, low, left))):
            rcopy(fwd.at[j, n], fwd.at[j, n], x_ss.at[j, n], x_rs.at[j, n], partner).wait_recv()
            own[j, s, part] = (own[j, s, part].astype(F32) + fwd[j, n].astype(F32)).astype(BF16)
            send(own.at[j, s, part], got.at[j, n, part], x_ss.at[j, 4 + n], x_rs.at[j, 4 + n], to)

    out_rows = (
        (pl.ds(0, full), pl.ds(pl.multiple_of(zh * full, 64), full)),
        (pl.ds(full, hid - full), pl.ds(pl.multiple_of(2 * full + zh * (hid - full), 64), hid - full)),
    )
    in_rows = (
        pl.ds(pl.multiple_of((1 - zh) * full, 64), full),
        pl.ds(pl.multiple_of(2 * full + (1 - zh) * (hid - full), 64), hid - full),
    )
    outs = {HIDDEN: out_d, GATE: out_g, UP: out_u}
    local = []

    def finish(j):
        which, other = JOBS[j]
        total = factors(j, x)
        for n, (a, b) in enumerate(((top, low), (low, top))):
            rcopy(got.at[j, n, b], got.at[j, n, b], x_ss.at[j, 2 + n], x_rs.at[j, 2 + n], partner).wait_recv()
            rcopy(got.at[j, n, a], got.at[j, n, a], x_ss.at[j, 4 + n], x_rs.at[j, 4 + n], partner).wait_recv()
        for n in range(2):
            total += got[j, n].astype(F32)
        for copy in opposite[j]:
            copy.wait_send()
        own[j, OPP] = (total * scale).astype(BF16)
        for n, (here, there) in enumerate(out_rows):
            if other:
                send(own.at[j, OPP, here], outs[which].at[there, :], z_ss.at[which, n], z_rs.at[which, n], across)
            else:
                copy = pltpu.make_async_copy(own.at[j, OPP, here], outs[which].at[there, :], loc_sem.at[which, n])
                copy.start()
                local.append(copy)

    multiply(0)
    multiply(1)

    loads[4].wait()
    loads[5].wait()

    def grad_piece(i, carry):
        span = pl.ds(pl.multiple_of(i * piece, piece), piece)
        slab = xg[1, span, :]
        for n in range(2):
            cols = pl.ds(n * piece, piece)
            back = nt(slab, wd[cols, :])
            gate_grad = (back * fa[span, cols].astype(F32)).astype(BF16)
            up_grad = (back * fb[span, cols].astype(F32)).astype(BF16)
            put_transposed(GATE, n, span, gate_grad)
            put_transposed(UP, n, span, up_grad)
            if n:
                lane = lax.broadcasted_iota(jnp.int32, (piece, piece), 1) - (full - piece)
                side = hid - full
                valid = (lane < 0) | ((lane >= side * zh) & (lane < side * (zh + 1)))
                gate_grad = jnp.where(valid, gate_grad, jnp.zeros_like(gate_grad))
                up_grad = jnp.where(valid, up_grad, jnp.zeros_like(up_grad))
            gu[0, span, cols] = gate_grad
            gu[1, span, cols] = up_grad
        return carry

    lax.fori_loop(0, pieces, grad_piece, 0)

    add_on(0)
    multiply(2)
    add_on(1)
    multiply(3)

    order = (2, 1, 3, 0)
    strip = 512

    def plane_rows(r):
        return pl.ds(pl.multiple_of(plane * ring(y, r), 16), plane)

    def staged(k):
        return wd.at[pl.ds(0, plane), pl.ds((k % 2) * half, half)]

    def back_piece(r, k, side, add):
        def one(n, carry):
            at = pl.ds(pl.multiple_of(side * half + n * strip, strip), strip)
            value = nt(gu[0, plane_rows(r), :], wg[at, :]) + nt(gu[1, plane_rows(r), :], wu[at, :])
            if add:
                value += pst[:, pl.ds(pl.multiple_of(n * strip, strip), strip)].astype(F32)
            wd[pl.ds(0, plane), pl.ds(pl.multiple_of((k % 2) * half + n * strip, strip), strip)] = value.astype(BF16)
            return carry

        lax.fori_loop(0, half // strip, one, 0)

    to_partner = []
    for k, r in enumerate(order):
        if k >= 2:
            to_partner[k - 2].wait_send()
        back_piece(r, k, 1 - c, False)
        copy = rcopy(staged(k), p_hbm.at[plane_rows(r), :], p_ss.at[k], p_rs.at[k], partner)
        copy.start()
        to_partner.append(copy)
    add_on(2)
    multiply(4)
    multiply(5)
    to_partner[2].wait_send()
    to_partner[3].wait_send()
    add_on(3)

    def spread(r):
        for rz in (2, 1, 3, 0):
            if r or rz:
                q = 4 * r + rz
                to = dev(0, ring(y, r), ring(z, rz), c)
                index = NZ * ring(y, r) + ring(z, rz)
                send(s_hbm.at[at_rows(index), :], r_hbm.at[q], r_ss.at[q], r_rs.at[q], to)

    written = []
    for k, r in enumerate(order):
        rcopy(staged(k), p_hbm.at[plane_rows(r), :], p_ss.at[k], p_rs.at[k], partner).wait_recv()
        fetch = pltpu.make_async_copy(p_hbm.at[plane_rows(r), :], pst, fetch_sem.at[0])
        fetch.start()
        fetch.wait()
        back_piece(r, k, c, True)
        copy = pltpu.make_async_copy(staged(k), s_hbm.at[plane_rows(r), :], fetch_sem.at[1])
        copy.start()
        copy.wait()
        spread(r)

    finish(0)
    add_on(4)
    finish(1)
    add_on(5)
    finish(2)
    finish(3)

    def held(k):
        return wd.at[pl.ds(chip * (k // 2), chip), pl.ds((k % 2) * half, half)]

    total = None
    for part in range(2):
        fetches = []
        for k in range(8):
            q = 8 * part + k
            if q:
                rcopy(r_hbm.at[q], r_hbm.at[q], r_ss.at[q], r_rs.at[q], partner).wait_recv()
                src = r_hbm.at[q]
            else:
                src = s_hbm.at[at_rows(me), :]
            fetches.append(pltpu.make_async_copy(src, held(k), fetch_sem.at[2 + k]))
            fetches[-1].start()
        for fetch in fetches:
            fetch.wait()
        for n in range(4):
            span = half // 4
            sum_ = None
            for k in range(8):
                at = pl.ds((k % 2) * half + n * span, span)
                term = wd[pl.ds(chip * (k // 2), chip), at].astype(F32)
                sum_ = term if sum_ is None else sum_ + term
            at = pl.ds(n * span, span)
            if part == 0:
                fin[0:chip, at] = sum_
            else:
                fin2[0:chip, at] = (fin[0:chip, at] + sum_).astype(BF16)

    mine = pl.ds(pl.multiple_of(c * half, half), half)
    theirs = pl.ds(pl.multiple_of((1 - c) * half, half), half)
    keep = fin2.at[pl.ds(pl.multiple_of(main * c, 16), main), :]
    give = fin2.at[pl.ds(pl.multiple_of(main * (1 - c), 16), main), :]
    ends = fin2.at[pl.ds(2 * main, 2 * rest), :]
    send(give, ig_main.at[:, mine], o_ss.at[0], o_rs.at[0], partner)
    send(ends, ig_tail.at[:, mine], o_ss.at[1], o_rs.at[1], partner)
    for n, (src, dst) in enumerate(((keep, ig_main.at[:, mine]), (ends, ig_tail.at[:, mine]))):
        copy = pltpu.make_async_copy(src, dst, fetch_sem.at[n])
        copy.start()
        local.append(copy)

    finish(4)
    finish(5)

    for n, (src, dst) in enumerate(((keep, ig_main), (ends, ig_tail))):
        rcopy(src, dst.at[:, theirs], o_ss.at[n], o_rs.at[n], partner).wait_recv()
    for which in (HIDDEN, GATE, UP):
        for n, (here, _) in enumerate(out_rows):
            rcopy(own.at[0, OPP, here], outs[which].at[in_rows[n], :], z_ss.at[which, n], z_rs.at[which, n], partner).wait_recv()
    for copy in pending:
        copy.wait_send()
    for copy in local:
        copy.wait()


def local(inputs, out_grad, w_gate, w_up, w_down):
    _, rows, width = inputs.shape
    units = w_gate.shape[1]
    hid = units // 2
    pad = hid + 64
    tokens = 2 * rows * NY * NZ
    half = width // 2
    block = width // 8
    chip = 2 * rows
    scale = 1.0 / math.sqrt(rows * lax.axis_size("tensor") * lax.axis_size("dp"))
    dma = pltpu.SemaphoreType.DMA
    any_ = pl.BlockSpec(memory_space=pl.ANY)
    vmem = pl.BlockSpec(memory_space=pltpu.VMEM)
    arr = lambda *shape: jax.ShapeDtypeStruct(shape, BF16)
    outs = pl.pallas_call(
        functools.partial(kernel, scale),
        out_shape=(
            arr(units, block), arr(units, block), arr(units, block),
            arr(rows // 16 * 16, width), arr(16, width),
            arr(tokens, half), arr(tokens, half), arr(NY * NZ, chip, half),
        ),
        in_specs=[vmem, vmem, any_, any_, any_],
        out_specs=(any_,) * 8,
        scratch_shapes=[
            pltpu.VMEM((2, tokens, width), BF16),
            pltpu.VMEM((width, pad), BF16),
            pltpu.VMEM((width, pad), BF16),
            pltpu.VMEM((pad, width), BF16),
            pltpu.VMEM((tokens, pad), BF16),
            pltpu.VMEM((tokens, pad), BF16),
            pltpu.VMEM((3, hid, tokens), BF16),
            pltpu.VMEM((2, tokens, pad), BF16),
            pltpu.VMEM((6, 3, hid, block), BF16),
            pltpu.VMEM((6, 2, hid // 2, block), BF16),
            pltpu.VMEM((6, 2, hid, block), BF16),
            pltpu.VMEM((NZ * chip, half), BF16),
            pltpu.VMEM((2, 16, width), BF16),
            pltpu.VMEM((2, 16, width), BF16),
            pltpu.VMEM((chip, half), F32),
            pltpu.VMEM((chip, half), BF16),
            dma((6,)), dma((2, 2)), dma((2, 2)),
            dma((2, 20)), dma((2, 20)), dma((2, 16)), dma((2, 16)),
            dma((6, 6)), dma((6, 6)),
            dma((4,)), dma((4,)), dma((16,)), dma((16,)),
            dma((3, 2)), dma((3, 2)), dma((2,)), dma((2,)),
            dma((3, 2)), dma((10,)),
        ],
        compiler_params=pltpu.CompilerParams(
            collective_id=0, has_side_effects=True, vmem_limit_bytes=63 * 2**20
        ),
        cost_estimate=pl.CostEstimate(
            flops=16 * tokens * width * hid, bytes_accessed=6 * width * units, transcendentals=tokens * hid
        ),
    )(inputs[0], out_grad[0], w_gate, w_up, w_down)
    grad_gate, grad_up, grad_down, ig_main, ig_tail = outs[:5]
    core = lax.rem(lax.axis_index("tensor"), 2)
    rest = rows - rows // 16 * 16
    ends = lax.dynamic_slice_in_dim(ig_tail, core * rest, rest, 0)
    input_grad = jnp.concatenate([ig_main, ends], axis=0)[None]
    return (input_grad, grad_gate.T, grad_up.T, grad_down)


def solution(mesh):
    placed = (
        P("dp", "tensor", None),
        P("dp", "tensor", None),
        P(None, "tensor"),
        P(None, "tensor"),
        P("tensor", None),
    )
    return jax.shard_map(
        local,
        mesh=mesh,
        in_specs=placed,
        out_specs=(
            P("dp", "tensor", None),
            P("dp", "tensor"),
            P("dp", "tensor"),
            P("tensor", "dp"),
        ),
        check_vma=False,
    )
```

time: 517 us -> 240 us (0.46)
  waiting for transfers between devices: 411 us -> 0 us
  Pallas kernels: 0 us -> 227 us
  matrix products: 80.8 us -> 0 us
  between operations: 14.1 us -> 0.65 us
    reduce_scatter x4 -> x0, waiting for transfers between devices: 348 us -> none  [the longest x1 107 us: local(): lax.psum_scatter(part_gate.astype(jnp.bfloat16), 'dp', scatter_dimension=...]
    pallas_call x0 -> x1, Pallas kernels: none -> 227 us  [local(): pl.pallas_call(functools.partial(kernel, scale), out_shape=(arr(units, bl...]
    dot_general x8 -> x0, matrix products: 80.8 us -> none  [the longest x3 30.5 us: contract_cols(): lax.dot_general(left, right, (((1,), (1,)), ((), ())), preferred_element_...]
    all_gather x2 -> x0, waiting for transfers between devices: 61.6 us -> none  [the longest x1 41.8 us: local(): lax.all_gather(inputs, 'tensor', axis=1, tiled=True)]
  transfers between devices with their start and end apart: 6 -> 0, of which waited for: 6 -> 0; matrix products, arithmetic and copies ran while one was open for 13% -> 0% of each run, Pallas kernels for 0% -> 0%
where the time goes in v1:
time: 240 us; the launch traced here: 237 us
  Pallas kernels  227 us (95%)
  local copies, waits for them, and re-layouts  7.43 us (3%)
    pallas_call x1, Pallas kernels, local(): pl.pallas_call(functools.partial(kernel, scale), out_shape=(arr(units, bl...  227 us
    unnamed x3, local copies, waits for them, and re-layouts  6.58 us

profile of v1, /device:TPU:64, one launch (start us, length us, event | category | flops | bytes accessed | tf_op | source)
XLA Modules:
  0.0 236.6 jit_solution(7532457559875376968)
XLA Ops:
  0.6 226.8 %shard_map.84 = (bf16[896,512]{1,0:T(8,128)(2,1)}, bf16[896,512]{1,0:T(8,128)(2,1)}, bf16[896,512]{1,0:T(8,128)(2,1)}, bf16[32,4096]{1,0:T(8,128)(2,1)}, bf16[16...) custom-call(bf16[40,4096]{1,0:T(8,128)(2,1)} %bitcast.8, ...), custom_call_target="tpu_custom_call" | custom-call | flops 37580963840 | bytes 22020096 | tf_op jit(solution)/shard_map/pallas_call | solution.py:501
  227.5 0.8 constant_dynamic-slice_fusion
  228.3 1.7 maximum_bitcast_fusion
  230.0 2.2 copy.9
  232.3 2.2 copy.10
  234.5 2.2 copy.12

commit v2 on v1

--- a/solution.py
+++ b/solution.py
@@ -13,7 +13,7 @@
 NX = NY = NZ = 4
 NT = (((1,), (1,)), ((), ()))
 HIDDEN, GATE, UP = 0, 1, 2
-JOBS = ((HIDDEN, True), (HIDDEN, False), (GATE, True), (UP, True), (GATE, False), (UP, False))
+JOBS = ((HIDDEN, True), (GATE, True), (UP, True), (HIDDEN, False), (GATE, False), (UP, False))
 
 
 def nt(left, right):
@@ -23,7 +23,7 @@
 def kernel(
     scale, x_in, g_in, wg_hbm, wu_hbm, wd_hbm,
     out_g, out_u, out_d, ig_main, ig_tail, p_hbm, s_hbm, r_hbm,
-    xg, wg, wu, wd, fa, fb, lt, gu, own, fwd, got, pst, tail, ptail, fin, fin2,
+    xg, wg, wu, wd, fa, fb, lt, gu, own, fwd, got, sums, tail, ptail,
     w_sem, core_ss, core_rs, ag_ss, ag_rs, sh_ss, sh_rs, x_ss, x_rs,
     p_ss, p_rs, r_ss, r_rs, z_ss, z_rs, o_ss, o_rs, loc_sem, fetch_sem,
 ):
@@ -334,7 +334,6 @@
                 local.append(copy)
 
     multiply(0)
-    multiply(1)
 
     loads[4].wait()
     loads[5].wait()
@@ -361,108 +360,123 @@
 
     lax.fori_loop(0, pieces, grad_piece, 0)
 
+    multiply(1)
     add_on(0)
     multiply(2)
+
+    order = (2, 1, 3, 0)
+    strip = 512
+    strips = half // strip
+
+    def back_piece(k, cc, add):
+        buf = (fa, fb)[k % 2]
+        uu, vv = frame(cc)
+        spans = [at_rows(slot(cc, ring(uu, order[k]), ring(vv, rv))) for rv in range(4)]
+
+        def one(n, carry):
+            at = pl.ds(pl.multiple_of(cc * half + n * strip, strip), strip)
+            held = pl.ds(pl.multiple_of(n * plane, 16), plane)
+            value = sum(
+                nt(jnp.concatenate([gu[w, span, :] for span in spans], axis=0), weight[at, :])
+                for w, weight in enumerate((wg, wu))
+            )
+            if add:
+                value += buf[held, :].astype(F32)
+                wd[0:plane, pl.ds(pl.multiple_of((k % 2) * half + n * strip, strip), strip)] = value.astype(BF16)
+            else:
+                buf[held, :] = value.astype(BF16)
+            return carry
+
+        lax.fori_loop(0, strips, one, 0)
+
+    to_partner = []
+    for k in range(4):
+        if k >= 2:
+            to_partner[k - 2].wait_send()
+        back_piece(k, 1 - c, False)
+        copy = rcopy((fa, fb)[k % 2], p_hbm.at[k], p_ss.at[k], p_rs.at[k], partner)
+        copy.start()
+        to_partner.append(copy)
     add_on(1)
     multiply(3)
-
-    order = (2, 1, 3, 0)
-    strip = 512
-
-    def plane_rows(r):
-        return pl.ds(pl.multiple_of(plane * ring(y, r), 16), plane)
-
-    def staged(k):
-        return wd.at[pl.ds(0, plane), pl.ds((k % 2) * half, half)]
-
-    def back_piece(r, k, side, add):
-        def one(n, carry):
-            at = pl.ds(pl.multiple_of(side * half + n * strip, strip), strip)
-            value = nt(gu[0, plane_rows(r), :], wg[at, :]) + nt(gu[1, plane_rows(r), :], wu[at, :])
-            if add:
-                value += pst[:, pl.ds(pl.multiple_of(n * strip, strip), strip)].astype(F32)
-            wd[pl.ds(0, plane), pl.ds(pl.multiple_of((k % 2) * half + n * strip, strip), strip)] = value.astype(BF16)
-            return carry
-
-        lax.fori_loop(0, half // strip, one, 0)
-
-    to_partner = []
-    for k, r in enumerate(order):
-        if k >= 2:
-            to_partner[k - 2].wait_send()
-        back_piece(r, k, 1 - c, False)
-        copy = rcopy(staged(k), p_hbm.at[plane_rows(r), :], p_ss.at[k], p_rs.at[k], partner)
+    to_partner[2].wait_send()
+    to_partner[3].wait_send()
+
+    def fetch(k):
+        rcopy(p_hbm.at[k], p_hbm.at[k], p_ss.at[k], p_rs.at[k], partner).wait_recv()
+        copy = pltpu.make_async_copy(p_hbm.at[k], (fa, fb)[k % 2], fetch_sem.at[k % 2])
         copy.start()
-        to_partner.append(copy)
+        return copy
+
+    def spread(k):
+        for rv in (2, 1, 3):
+            q = 3 * k + rv - 1
+            src = s_hbm.at[k, pl.ds(chip * rv, chip), :]
+            send(src, r_hbm.at[q], r_ss.at[q], r_rs.at[q], uv_dev(u, ring(v, rv)))
+
+    fetched = [fetch(0), fetch(1)]
+    written = []
+    for k in range(4):
+        fetched[k].wait()
+        back_piece(k, c, True)
+        copy = pltpu.make_async_copy(
+            wd.at[pl.ds(0, plane), pl.ds((k % 2) * half, half)], s_hbm.at[k], fetch_sem.at[2 + k % 2]
+        )
+        copy.start()
+        written.append(copy)
+        if k + 2 < 4:
+            fetched.append(fetch(k + 2))
+        if k:
+            written[k - 1].wait()
+            spread(k - 1)
+    written[3].wait()
+    spread(3)
+
     add_on(2)
     multiply(4)
+    add_on(3)
     multiply(5)
-    to_partner[2].wait_send()
-    to_partner[3].wait_send()
-    add_on(3)
-
-    def spread(r):
-        for rz in (2, 1, 3, 0):
-            if r or rz:
-                q = 4 * r + rz
-                to = dev(0, ring(y, r), ring(z, rz), c)
-                index = NZ * ring(y, r) + ring(z, rz)
-                send(s_hbm.at[at_rows(index), :], r_hbm.at[q], r_ss.at[q], r_rs.at[q], to)
-
-    written = []
-    for k, r in enumerate(order):
-        rcopy(staged(k), p_hbm.at[plane_rows(r), :], p_ss.at[k], p_rs.at[k], partner).wait_recv()
-        fetch = pltpu.make_async_copy(p_hbm.at[plane_rows(r), :], pst, fetch_sem.at[0])
-        fetch.start()
-        fetch.wait()
-        back_piece(r, k, c, True)
-        copy = pltpu.make_async_copy(staged(k), s_hbm.at[plane_rows(r), :], fetch_sem.at[1])
-        copy.start()
-        copy.wait()
-        spread(r)
-
     finish(0)
+    finish(1)
+
+    def collect(arrivals, kept, k):
+        places = [
+            wd.at[pl.ds(chip * (n // 2 + 2 * (k % 2)), chip), pl.ds((n % 2) * half, half)] for n in range(4)
+        ]
+        copies = []
+        for n, q in enumerate(arrivals):
+            rcopy(r_hbm.at[q], r_hbm.at[q], r_ss.at[q], r_rs.at[q], partner).wait_recv()
+            copies.append(pltpu.make_async_copy(r_hbm.at[q], places[n], fetch_sem.at[4 + n]))
+        if kept is not None:
+            copies.append(pltpu.make_async_copy(kept, places[3], fetch_sem.at[7]))
+        for copy in copies:
+            copy.start()
+        for copy in copies:
+            copy.wait()
+        span = half // 4
+        for n in range(4):
+            at = pl.ds(n * span, span)
+            terms = [place[:, at].astype(F32) for place in places[:len(copies)]]
+            if kept is None:
+                terms.append(sums[3, :, at].astype(F32))
+            sums[k, :, at] = sum(terms).astype(BF16)
+
+    for k in range(4):
+        collect([3 * k, 3 * k + 1, 3 * k + 2], s_hbm.at[k, pl.ds(0, chip), :], k)
+        r = order[k]
+        if r:
+            q = 11 + r
+            send(sums.at[k], r_hbm.at[q], r_ss.at[q], r_rs.at[q], uv_dev(ring(u, r), v))
     add_on(4)
-    finish(1)
+    finish(2)
     add_on(5)
-    finish(2)
-    finish(3)
-
-    def held(k):
-        return wd.at[pl.ds(chip * (k // 2), chip), pl.ds((k % 2) * half, half)]
-
-    total = None
-    for part in range(2):
-        fetches = []
-        for k in range(8):
-            q = 8 * part + k
-            if q:
-                rcopy(r_hbm.at[q], r_hbm.at[q], r_ss.at[q], r_rs.at[q], partner).wait_recv()
-                src = r_hbm.at[q]
-            else:
-                src = s_hbm.at[at_rows(me), :]
-            fetches.append(pltpu.make_async_copy(src, held(k), fetch_sem.at[2 + k]))
-            fetches[-1].start()
-        for fetch in fetches:
-            fetch.wait()
-        for n in range(4):
-            span = half // 4
-            sum_ = None
-            for k in range(8):
-                at = pl.ds((k % 2) * half + n * span, span)
-                term = wd[pl.ds(chip * (k // 2), chip), at].astype(F32)
-                sum_ = term if sum_ is None else sum_ + term
-            at = pl.ds(n * span, span)
-            if part == 0:
-                fin[0:chip, at] = sum_
-            else:
-                fin2[0:chip, at] = (fin[0:chip, at] + sum_).astype(BF16)
+    collect([12, 13, 14], None, 4)
 
     mine = pl.ds(pl.multiple_of(c * half, half), half)
     theirs = pl.ds(pl.multiple_of((1 - c) * half, half), half)
-    keep = fin2.at[pl.ds(pl.multiple_of(main * c, 16), main), :]
-    give = fin2.at[pl.ds(pl.multiple_of(main * (1 - c), 16), main), :]
-    ends = fin2.at[pl.ds(2 * main, 2 * rest), :]
+    keep = sums.at[4, pl.ds(pl.multiple_of(main * c, 16), main), :]
+    give = sums.at[4, pl.ds(pl.multiple_of(main * (1 - c), 16), main), :]
+    ends = sums.at[4, pl.ds(2 * main, 2 * rest), :]
     send(give, ig_main.at[:, mine], o_ss.at[0], o_rs.at[0], partner)
     send(ends, ig_tail.at[:, mine], o_ss.at[1], o_rs.at[1], partner)
     for n, (src, dst) in enumerate(((keep, ig_main.at[:, mine]), (ends, ig_tail.at[:, mine]))):
@@ -470,6 +484,7 @@
         copy.start()
         local.append(copy)
 
+    finish(3)
     finish(4)
     finish(5)
 
@@ -482,6 +497,22 @@
         copy.wait_send()
     for copy in local:
         copy.wait()
+
+
+def arrange(gate_t, up_t, down, ig_main, ig_tail, grad_gate, grad_up, grad_down, input_grad, sem):
+    move = pltpu.make_async_copy(down, grad_down, sem)
+    move.start()
+    main = ig_main.shape[0]
+    rest = input_grad.shape[0] - main
+    core = lax.rem(lax.axis_index("tensor"), 2)
+    ends = ig_tail[...].astype(F32)
+    input_grad[0:main, :] = ig_main[...]
+    input_grad[main:, :] = jnp.where(core == 0, ends[0:rest], ends[rest:]).astype(BF16)
+    for n in range(gate_t.shape[0] // 128):
+        at = pl.ds(n * 128, 128)
+        grad_gate[:, at] = gate_t[at, :].T
+        grad_up[:, at] = up_t[at, :].T
+    move.wait()
 
 
 def local(inputs, out_grad, w_gate, w_up, w_down):
@@ -503,7 +534,7 @@
         out_shape=(
             arr(units, block), arr(units, block), arr(units, block),
             arr(rows // 16 * 16, width), arr(16, width),
-            arr(tokens, half), arr(tokens, half), arr(NY * NZ, chip, half),
+            arr(4, tokens, half // 4), arr(4, tokens // 4, half), arr(NY * NZ - 1, chip, half),
         ),
         in_specs=[vmem, vmem, any_, any_, any_],
         out_specs=(any_,) * 8,
@@ -519,17 +550,15 @@
             pltpu.VMEM((6, 3, hid, block), BF16),
             pltpu.VMEM((6, 2, hid // 2, block), BF16),
             pltpu.VMEM((6, 2, hid, block), BF16),
-            pltpu.VMEM((NZ * chip, half), BF16),
+            pltpu.VMEM((5, chip, half), BF16),
             pltpu.VMEM((2, 16, width), BF16),
             pltpu.VMEM((2, 16, width), BF16),
-            pltpu.VMEM((chip, half), F32),
-            pltpu.VMEM((chip, half), BF16),
             dma((6,)), dma((2, 2)), dma((2, 2)),
             dma((2, 20)), dma((2, 20)), dma((2, 16)), dma((2, 16)),
             dma((6, 6)), dma((6, 6)),
-            dma((4,)), dma((4,)), dma((16,)), dma((16,)),
+            dma((4,)), dma((4,)), dma((15,)), dma((15,)),
             dma((3, 2)), dma((3, 2)), dma((2,)), dma((2,)),
-            dma((3, 2)), dma((10,)),
+            dma((3, 2)), dma((8,)),
         ],
         compiler_params=pltpu.CompilerParams(
             collective_id=0, has_side_effects=True, vmem_limit_bytes=63 * 2**20
@@ -538,12 +567,14 @@
             flops=16 * tokens * width * hid, bytes_accessed=6 * width * units, transcendentals=tokens * hid
         ),
     )(inputs[0], out_grad[0], w_gate, w_up, w_down)
-    grad_gate, grad_up, grad_down, ig_main, ig_tail = outs[:5]
-    core = lax.rem(lax.axis_index("tensor"), 2)
-    rest = rows - rows // 16 * 16
-    ends = lax.dynamic_slice_in_dim(ig_tail, core * rest, rest, 0)
-    input_grad = jnp.concatenate([ig_main, ends], axis=0)[None]
-    return (input_grad, grad_gate.T, grad_up.T, grad_down)
+    grad_gate, grad_up, grad_down, input_grad = pl.pallas_call(
+        arrange,
+        out_shape=(arr(block, units), arr(block, units), arr(units, block), arr(rows, width)),
+        in_specs=[vmem, vmem, any_, vmem, vmem],
+        out_specs=(vmem, vmem, any_, vmem),
+        scratch_shapes=[dma(())],
+    )(*outs[:5])
+    return (input_grad[None], grad_gate, grad_up, grad_down)
 
 
 def solution(mesh):

time: 240 us -> 214 us (0.89)
  Pallas kernels: 227 us -> 210 us
  local copies, waits for them, and re-layouts: 7.43 us -> 0 us
    pallas_call x1, Pallas kernels: 227 us -> 178 us  [local(): pl.pallas_call(functools.partial(kernel, scale), out_shape=(arr(units, bl...]
    pallas_call x0 -> x1, Pallas kernels: none -> 31.8 us  [local(): pl.pallas_call(arrange, out_shape=(arr(block, units), arr(block, units),...]
    unnamed x3 -> x0, local copies, waits for them, and re-layouts: 6.58 us -> none
where the time goes in v2:
time: 214 us; the launch traced here: 211 us
  Pallas kernels  210 us (98%)
    pallas_call x1, Pallas kernels, local(): pl.pallas_call(functools.partial(kernel, scale), out_shape=(arr(units, bl...  178 us
    pallas_call x1, Pallas kernels, local(): pl.pallas_call(arrange, out_shape=(arr(block, units), arr(block, units),...  31.8 us

profile of v2, /device:TPU:64, one launch (start us, length us, event | category | flops | bytes accessed | tf_op | source)
XLA Modules:
  0.0 211.0 jit_solution(13097313503928958292)
XLA Ops:
  0.6 178.4 %shard_map.84 = (bf16[896,512]{1,0:T(8,128)(2,1)}, bf16[896,512]{1,0:T(8,128)(2,1)}, bf16[896,512]{1,0:T(8,128)(2,1)}, bf16[32,4096]{1,0:T(8,128)(2,1)}, bf16[16...) custom-call(bf16[40,4096]{1,0:T(8,128)(2,1)} %bitcast.3, ...), custom_call_target="tpu_custom_call" | custom-call | flops 37580963840 | bytes 22020096 | tf_op jit(solution)/shard_map/pallas_call | solution.py:532
  179.0 31.8 %shard_map.85 = (bf16[512,896]{1,0:T(8,128)(2,1)}, bf16[512,896]{1,0:T(8,128)(2,1)}, bf16[896,512]{1,0:T(8,128)(2,1)}, bf16[40,4096]{1,0:T(8,128)(2,1)}) custom-call(bf16[896,512]{1,0:T(8,128)(2,1)} %get-tuple-element.13.gate_t, bf16[896,512]{1,0:T(8,128)(2,1)} %get-tuple-element.14.up_t, bf16[896,512]{1,0:T(8,128)(2,1)} %get-tuple-element.15.down, ...), custom_call_target="tpu_custom_call" | custom-call | tf_op jit(solution)/shard_map/pallas_call | solution.py:570

commit v3 on v2

--- a/solution.py
+++ b/solution.py
@@ -13,7 +13,9 @@
 NX = NY = NZ = 4
 NT = (((1,), (1,)), ((), ()))
 HIDDEN, GATE, UP = 0, 1, 2
-JOBS = ((HIDDEN, True), (GATE, True), (UP, True), (HIDDEN, False), (GATE, False), (UP, False))
+LOW, HIGH, OTHER, SAME = 0, 1, 2, 3
+JOBS = ((HIDDEN, LOW), (HIDDEN, HIGH), (GATE, OTHER), (UP, OTHER), (GATE, SAME), (UP, SAME))
+PARTS = ((0, 0, 2), (1, 0, 1), (1, 2, 1))
 
 
 def nt(left, right):
@@ -23,7 +25,7 @@
 def kernel(
     scale, x_in, g_in, wg_hbm, wu_hbm, wd_hbm,
     out_g, out_u, out_d, ig_main, ig_tail, p_hbm, s_hbm, r_hbm,
-    xg, wg, wu, wd, fa, fb, lt, gu, own, fwd, got, sums, tail, ptail,
+    xg, wg, wu, wd, fa, fb, lt, gu, own, fwd, got, sums, pst, tail, ptail,
     w_sem, core_ss, core_rs, ag_ss, ag_rs, sh_ss, sh_rs, x_ss, x_rs,
     p_ss, p_rs, r_ss, r_rs, z_ss, z_rs, o_ss, o_rs, loc_sem, fetch_sem,
 ):
@@ -127,18 +129,17 @@
     pu, pv = frame(1 - c)
     GROUPS = (0, -1, 1, 2)
 
-    def region(a, ou, ov, part=None):
-        col = c * half if part is None else c * half + part * quarter
-        return xg.at[
-            a, at_rows(slot(c, ring(u, ou), ring(v, ov))),
-            pl.ds(pl.multiple_of(col, quarter), half if part is None else quarter),
-        ]
-
-    def partner_region(a, ou, ov):
-        return xg.at[
-            a, at_rows(slot(1 - c, ring(pu, ou), ring(pv, ov))),
-            pl.ds(pl.multiple_of((1 - c) * half, quarter), half),
-        ]
+    def columns(w, cc, part=None):
+        slab, start, count = PARTS[w]
+        size = count * quarter if part is None else count * quarter // 2
+        col = start * quarter + cc * count * quarter + (0 if part is None else part * size)
+        return pl.ds(pl.multiple_of(col, 512), size)
+
+    def region(w, ou, ov, part=None):
+        return xg.at[PARTS[w][0], at_rows(slot(c, ring(u, ou), ring(v, ov))), columns(w, c, part)]
+
+    def partner_region(w, ou, ov):
+        return xg.at[PARTS[w][0], at_rows(slot(1 - c, ring(pu, ou), ring(pv, ov))), columns(w, 1 - c)]
 
     def place(label):
         if label < 4:
@@ -171,10 +172,11 @@
 
     def gather_steps(a):
         def begin():
-            mine = xg.at[a, at_rows(me, main, main * (1 - c)), :]
-            rcopy(mine, mine, core_ss.at[a, 0], core_rs.at[a, 0], partner).wait_recv()
-            rcopy(tail.at[a], ptail.at[a], core_ss.at[a, 1], core_rs.at[a, 1], partner).wait_recv()
-            xg[a, at_rows(me, 2 * rest, 2 * main), :] = tail[a] + ptail[a]
+            if a < 2:
+                mine = xg.at[a, at_rows(me, main, main * (1 - c)), :]
+                rcopy(mine, mine, core_ss.at[a, 0], core_rs.at[a, 0], partner).wait_recv()
+                rcopy(tail.at[a], ptail.at[a], core_ss.at[a, 1], core_rs.at[a, 1], partner).wait_recv()
+                xg[a, at_rows(me, 2 * rest, 2 * main), :] = tail[a] + ptail[a]
             where = region(a, 0, 0)
             pass_on(a, 0, where, u_plus)
             pass_on(a, 1, where, u_minus)
@@ -220,16 +222,14 @@
         steps += [functools.partial(v_last, 3), take]
         return steps
 
-    steps_x, steps_g = gather_steps(0), gather_steps(1)
-    steps_x[0]()
-    steps_g[0]()
-    for step in steps_x[1:4]:
-        step()
-    for step in steps_g[1:4]:
-        step()
-    for step in steps_x[4:]:
-        step()
-    later = steps_g[4:]
+    steps_x, steps_a, steps_b = gather_steps(0), gather_steps(1), gather_steps(2)
+
+    def run(steps):
+        for step in steps:
+            step()
+
+    run(steps_x[:4] + steps_a[:1] + steps_x[4:8] + steps_a[1:4] + steps_x[8:])
+    later = steps_a[4:9] + steps_b[:1] + steps_a[9:]
 
     for load in loads[:4]:
         load.wait()
@@ -247,31 +247,30 @@
                 zh == 0, turned[keep:keep + side], turned[keep + side:keep + 2 * side]
             )
 
-    def gate_piece(i):
+    def gate_piece(i, n):
         span = pl.ds(pl.multiple_of(i * piece, piece), piece)
         slab = xg[0, span, :]
-        for n in range(2):
-            cols = pl.ds(n * piece, piece)
-            gate = jnp.dot(slab, wg[:, cols], preferred_element_type=F32)
-            up = jnp.dot(slab, wu[:, cols], preferred_element_type=F32)
-            sig = jax.nn.sigmoid(gate)
-            act = gate * sig
-            fb[span, cols] = act.astype(BF16)
-            fa[span, cols] = (up * sig * (1.0 + gate * (1.0 - sig))).astype(BF16)
-            put_transposed(HIDDEN, n, span, (act * up).astype(BF16))
+        cols = pl.ds(n * piece, piece)
+        gate = jnp.dot(slab, wg[:, cols], preferred_element_type=F32)
+        up = jnp.dot(slab, wu[:, cols], preferred_element_type=F32)
+        sig = jax.nn.sigmoid(gate)
+        act = gate * sig
+        fb[span, cols] = act.astype(BF16)
+        fa[span, cols] = (up * sig * (1.0 + gate * (1.0 - sig))).astype(BF16)
+        put_transposed(HIDDEN, n, span, (act * up).astype(BF16))
 
     pieces = tokens // piece
     done = 0
     for i in range(pieces):
-        gate_piece(i)
-        until = len(later) * (i + 1) // pieces
-        for step in later[done:until]:
-            step()
-        done = until
+        for n in range(2):
+            gate_piece(i, n)
+            until = len(later) * (2 * i + n + 1) // (2 * pieces)
+            run(later[done:until])
+            done = until
 
     def factors(j, xx):
-        which, other = JOBS[j]
-        side = 1 - zh if other else zh
+        which, side = JOBS[j]
+        side = (0, 1, 1 - zh, zh)[side]
         col = pl.multiple_of(side * half + lax.rem(xx, NX) * block, block)
         return jnp.dot(
             lt[which], xg[1 if which == HIDDEN else 0, :, pl.ds(col, block)],
@@ -287,13 +286,22 @@
             own[j, s] = factors(j, x + 1 + s).astype(BF16)
             return carry
 
-        lax.fori_loop(0, 3, one, 0)
-        opposite[j] = [
-            rcopy(own.at[j, OPP, top], fwd.at[j, 0], x_ss.at[j, 0], x_rs.at[j, 0], right),
-            rcopy(own.at[j, OPP, low], fwd.at[j, 1], x_ss.at[j, 1], x_rs.at[j, 1], left),
-        ]
-        for copy in opposite[j]:
-            copy.start()
+        def send_opposite():
+            opposite[j] = [
+                rcopy(own.at[j, OPP, top], fwd.at[j, 0], x_ss.at[j, 0], x_rs.at[j, 0], right),
+                rcopy(own.at[j, OPP, low], fwd.at[j, 1], x_ss.at[j, 1], x_rs.at[j, 1], left),
+            ]
+            for copy in opposite[j]:
+                copy.start()
+
+        if j == 0:
+            one(OPP, 0)
+            send_opposite()
+            one(R, 0)
+            one(L, 0)
+        else:
+            lax.fori_loop(0, 3, one, 0)
+            send_opposite()
         send(own.at[j, R, low], got.at[j, 0, low], x_ss.at[j, 2], x_rs.at[j, 2], right)
         send(own.at[j, L, top], got.at[j, 1, top], x_ss.at[j, 3], x_rs.at[j, 3], left)
 
@@ -314,26 +322,43 @@
     outs = {HIDDEN: out_d, GATE: out_g, UP: out_u}
     local = []
 
+    def prepare(j):
+        for copy in opposite[j]:
+            copy.wait_send()
+        own[j, OPP] = factors(j, x).astype(BF16)
+
     def finish(j):
-        which, other = JOBS[j]
-        total = factors(j, x)
+        which, side = JOBS[j]
         for n, (a, b) in enumerate(((top, low), (low, top))):
             rcopy(got.at[j, n, b], got.at[j, n, b], x_ss.at[j, 2 + n], x_rs.at[j, 2 + n], partner).wait_recv()
             rcopy(got.at[j, n, a], got.at[j, n, a], x_ss.at[j, 4 + n], x_rs.at[j, 4 + n], partner).wait_recv()
-        for n in range(2):
-            total += got[j, n].astype(F32)
-        for copy in opposite[j]:
-            copy.wait_send()
+        total = own[j, OPP].astype(F32) + got[j, 0].astype(F32) + got[j, 1].astype(F32)
         own[j, OPP] = (total * scale).astype(BF16)
         for n, (here, there) in enumerate(out_rows):
-            if other:
-                send(own.at[j, OPP, here], outs[which].at[there, :], z_ss.at[which, n], z_rs.at[which, n], across)
+            src, dst = own.at[j, OPP, here], outs[which].at[there, :]
+            def away():
+                return rcopy(src, dst, z_ss.at[which, n], z_rs.at[which, n], across)
+
+            def stay():
+                return pltpu.make_async_copy(src, dst, loc_sem.at[which, n])
+
+            if side == OTHER:
+                away().start()
+            elif side == SAME:
+                stay().start()
             else:
-                copy = pltpu.make_async_copy(own.at[j, OPP, here], outs[which].at[there, :], loc_sem.at[which, n])
-                copy.start()
-                local.append(copy)
+                pl.when(zh != side)(lambda: away().start())
+                pl.when(zh == side)(lambda: stay().start())
+            if side in (OTHER, LOW):
+                pending.append(away())
+            if side in (SAME, HIGH):
+                local.append(stay())
 
     multiply(0)
+    run(steps_b[1:10])
+    add_on(0)
+    run(steps_b[10:])
+    multiply(1)
 
     loads[4].wait()
     loads[5].wait()
@@ -360,9 +385,9 @@
 
     lax.fori_loop(0, pieces, grad_piece, 0)
 
-    multiply(1)
-    add_on(0)
+    add_on(1)
     multiply(2)
+    prepare(0)
 
     order = (2, 1, 3, 0)
     strip = 512
@@ -381,7 +406,7 @@
                 for w, weight in enumerate((wg, wu))
             )
             if add:
-                value += buf[held, :].astype(F32)
+                value += pst[k % 2, held, :].astype(F32)
                 wd[0:plane, pl.ds(pl.multiple_of((k % 2) * half + n * strip, strip), strip)] = value.astype(BF16)
             else:
                 buf[held, :] = value.astype(BF16)
@@ -390,21 +415,18 @@
         lax.fori_loop(0, strips, one, 0)
 
     to_partner = []
-    for k in range(4):
+
+    def give_piece(k):
         if k >= 2:
             to_partner[k - 2].wait_send()
         back_piece(k, 1 - c, False)
         copy = rcopy((fa, fb)[k % 2], p_hbm.at[k], p_ss.at[k], p_rs.at[k], partner)
         copy.start()
         to_partner.append(copy)
-    add_on(1)
-    multiply(3)
-    to_partner[2].wait_send()
-    to_partner[3].wait_send()
 
     def fetch(k):
         rcopy(p_hbm.at[k], p_hbm.at[k], p_ss.at[k], p_rs.at[k], partner).wait_recv()
-        copy = pltpu.make_async_copy(p_hbm.at[k], (fa, fb)[k % 2], fetch_sem.at[k % 2])
+        copy = pltpu.make_async_copy(p_hbm.at[k], pst.at[k % 2], fetch_sem.at[k % 2])
         copy.start()
         return copy
 
@@ -414,30 +436,53 @@
             src = s_hbm.at[k, pl.ds(chip * rv, chip), :]
             send(src, r_hbm.at[q], r_ss.at[q], r_rs.at[q], uv_dev(u, ring(v, rv)))
 
-    fetched = [fetch(0), fetch(1)]
     written = []
-    for k in range(4):
-        fetched[k].wait()
+
+    def sum_piece(k, fetched):
+        fetched.wait()
         back_piece(k, c, True)
         copy = pltpu.make_async_copy(
             wd.at[pl.ds(0, plane), pl.ds((k % 2) * half, half)], s_hbm.at[k], fetch_sem.at[2 + k % 2]
         )
         copy.start()
         written.append(copy)
-        if k + 2 < 4:
-            fetched.append(fetch(k + 2))
-        if k:
-            written[k - 1].wait()
-            spread(k - 1)
-    written[3].wait()
-    spread(3)
-
+
+    def send_piece(k):
+        written[k].wait()
+        spread(k)
+
+    give_piece(0)
+    give_piece(1)
+    finish(0)
+    p0 = fetch(0)
+    give_piece(2)
+    sum_piece(0, p0)
+    p1 = fetch(1)
+    multiply(3)
+    send_piece(0)
+    sum_piece(1, p1)
     add_on(2)
+    give_piece(3)
+    send_piece(1)
+    p2 = fetch(2)
+    prepare(1)
+    finish(1)
+    p3 = fetch(3)
+    sum_piece(2, p2)
+    prepare(2)
+    send_piece(2)
+    sum_piece(3, p3)
+    add_on(3)
+    send_piece(3)
     multiply(4)
-    add_on(3)
     multiply(5)
-    finish(0)
-    finish(1)
+    to_partner[2].wait_send()
+    to_partner[3].wait_send()
+    finish(2)
+    prepare(3)
+    prepare(4)
+    add_on(4)
+    finish(3)
 
     def collect(arrivals, kept, k):
         places = [
@@ -467,8 +512,7 @@
         if r:
             q = 11 + r
             send(sums.at[k], r_hbm.at[q], r_ss.at[q], r_rs.at[q], uv_dev(ring(u, r), v))
-    add_on(4)
-    finish(2)
+    prepare(5)
     add_on(5)
     collect([12, 13, 14], None, 4)
 
@@ -484,7 +528,6 @@
         copy.start()
         local.append(copy)
 
-    finish(3)
     finish(4)
     finish(5)
 
@@ -499,9 +542,7 @@
         copy.wait()
 
 
-def arrange(gate_t, up_t, down, ig_main, ig_tail, grad_gate, grad_up, grad_down, input_grad, sem):
-    move = pltpu.make_async_copy(down, grad_down, sem)
-    move.start()
+def arrange(gate_t, up_t, down, ig_main, ig_tail, grad_gate, grad_up, grad_down, input_grad):
     main = ig_main.shape[0]
     rest = input_grad.shape[0] - main
     core = lax.rem(lax.axis_index("tensor"), 2)
@@ -512,7 +553,7 @@
         at = pl.ds(n * 128, 128)
         grad_gate[:, at] = gate_t[at, :].T
         grad_up[:, at] = up_t[at, :].T
-    move.wait()
+    grad_down[...] = down[...]
 
 
 def local(inputs, out_grad, w_gate, w_up, w_down):
@@ -551,10 +592,11 @@
             pltpu.VMEM((6, 2, hid // 2, block), BF16),
             pltpu.VMEM((6, 2, hid, block), BF16),
             pltpu.VMEM((5, chip, half), BF16),
+            pltpu.VMEM((2, tokens, half // 4), BF16),
             pltpu.VMEM((2, 16, width), BF16),
             pltpu.VMEM((2, 16, width), BF16),
             dma((6,)), dma((2, 2)), dma((2, 2)),
-            dma((2, 20)), dma((2, 20)), dma((2, 16)), dma((2, 16)),
+            dma((3, 20)), dma((3, 20)), dma((3, 16)), dma((3, 16)),
             dma((6, 6)), dma((6, 6)),
             dma((4,)), dma((4,)), dma((15,)), dma((15,)),
             dma((3, 2)), dma((3, 2)), dma((2,)), dma((2,)),
@@ -570,9 +612,8 @@
     grad_gate, grad_up, grad_down, input_grad = pl.pallas_call(
         arrange,
         out_shape=(arr(block, units), arr(block, units), arr(units, block), arr(rows, width)),
-        in_specs=[vmem, vmem, any_, vmem, vmem],
-        out_specs=(vmem, vmem, any_, vmem),
-        scratch_shapes=[dma(())],
+        in_specs=[vmem] * 5,
+        out_specs=(vmem,) * 4,
     )(*outs[:5])
     return (input_grad[None], grad_gate, grad_up, grad_down)
 

time: 214 us -> 186 us (0.87); the launches traced: 211 us -> 186 us
  Pallas kernels: 210 us -> 185 us
    pallas_call x1, Pallas kernels: 31.8 us -> 3.97 us  [local(): pl.pallas_call(arrange, out_shape=(arr(block, units), arr(block, units),...]
    pallas_call x1, Pallas kernels: 178 us -> 181 us  [local(): pl.pallas_call(functools.partial(kernel, scale), out_shape=(arr(units, bl...]
where the time goes in v3:
time: 186 us
  Pallas kernels  185 us (99%)
    pallas_call x1, Pallas kernels, local(): pl.pallas_call(functools.partial(kernel, scale), out_shape=(arr(units, bl...  181 us
    pallas_call x1, Pallas kernels, local(): pl.pallas_call(arrange, out_shape=(arr(block, units), arr(block, units),...  3.97 us

profile of v3, /device:TPU:64, one launch (start us, length us, event | category | flops | bytes accessed | tf_op | source)
XLA Modules:
  0.0 185.6 jit_solution(17143731769723453921)
XLA Ops:
  0.6 180.9 %shard_map.84 = (bf16[896,512]{1,0:T(8,128)(2,1)}, bf16[896,512]{1,0:T(8,128)(2,1)}, bf16[896,512]{1,0:T(8,128)(2,1)}, bf16[32,4096]{1,0:T(8,128)(2,1)}, bf16[16...) custom-call(bf16[40,4096]{1,0:T(8,128)(2,1)} %bitcast.3, ...), custom_call_target="tpu_custom_call" | custom-call | flops 37580963840 | bytes 22020096 | tf_op jit(solution)/shard_map/pallas_call | solution.py:573
  181.6 4.0 %shard_map.85 = (bf16[512,896]{1,0:T(8,128)(2,1)}, bf16[512,896]{1,0:T(8,128)(2,1)}, bf16[896,512]{1,0:T(8,128)(2,1)}, bf16[40,4096]{1,0:T(8,128)(2,1)}) custom-call(bf16[896,512]{1,0:T(8,128)(2,1)} %get-tuple-element.13.gate_t, bf16[896,512]{1,0:T(8,128)(2,1)} %get-tuple-element.14.up_t, bf16[896,512]{1,0:T(8,128)(2,1)} %get-tuple-element.15.down, ...), custom_call_target="tpu_custom_call" | custom-call | tf_op jit(solution)/shard_map/pallas_call | solution.py:612

commit v4 on v3

--- a/solution.py
+++ b/solution.py
@@ -214,22 +214,23 @@
                         where = partner_region(a, ou, ov)
                         rcopy(where, where, sh_ss.at[a, n], sh_rs.at[a, n], partner).wait_recv()
 
-        steps = [begin, functools.partial(u_step, 0), functools.partial(u_step, 1), u_last]
+        steps = {"begin": begin, "u0": functools.partial(u_step, 0), "u1": functools.partial(u_step, 1)}
+        steps.update(ulast=u_last, take=take)
         for r in range(4):
-            steps += [functools.partial(v_step, r, 0), functools.partial(v_step, r, 1)]
-            if r:
-                steps.append(functools.partial(v_last, r - 1))
-        steps += [functools.partial(v_last, 3), take]
+            for kind in range(2):
+                steps[f"v{r}{kind}"] = functools.partial(v_step, r, kind)
+            steps[f"vl{r}"] = functools.partial(v_last, r)
         return steps
 
-    steps_x, steps_a, steps_b = gather_steps(0), gather_steps(1), gather_steps(2)
-
-    def run(steps):
-        for step in steps:
-            step()
-
-    run(steps_x[:4] + steps_a[:1] + steps_x[4:8] + steps_a[1:4] + steps_x[8:])
-    later = steps_a[4:9] + steps_b[:1] + steps_a[9:]
+    steps = [gather_steps(w) for w in range(len(PARTS))]
+
+    def go(w, *names):
+        for name in names:
+            steps[w][name]()
+
+    go(0, "begin", "u0", "u1", "v00", "v01", "ulast", "v10", "v11", "v20", "v21", "vl0", "v30", "v31", "vl1", "vl2")
+    go(1, "begin")
+    go(0, "vl3", "take")
 
     for load in loads[:4]:
         load.wait()
@@ -260,13 +261,32 @@
         put_transposed(HIDDEN, n, span, (act * up).astype(BF16))
 
     pieces = tokens // piece
-    done = 0
-    for i in range(pieces):
-        for n in range(2):
-            gate_piece(i, n)
-            until = len(later) * (2 * i + n + 1) // (2 * pieces)
-            run(later[done:until])
-            done = until
+    gates = [(i, n) for i in range(pieces) for n in range(2)]
+
+    def gate(count):
+        for _ in range(count):
+            gate_piece(*gates.pop(0))
+
+    gate(2)
+    go(1, "u0", "u1", "v00", "v01")
+    gate(2)
+    go(1, "ulast", "v10", "v11")
+    go(2, "begin")
+    gate(1)
+    go(1, "v20", "v21", "vl0")
+    gate(2)
+    go(1, "v30", "v31")
+    go(2, "u0")
+    go(1, "vl1")
+    go(2, "u1")
+    gate(1)
+    go(2, "v00", "v01")
+    gate(1)
+    go(1, "vl2", "vl3")
+    go(2, "ulast")
+    gate(len(gates))
+    go(2, "v10", "v11")
+    go(1, "take")
 
     def factors(j, xx):
         which, side = JOBS[j]
@@ -281,29 +301,30 @@
     R, OPP, L = 0, 1, 2
     opposite = {}
 
-    def multiply(j):
-        def one(s, carry):
-            own[j, s] = factors(j, x + 1 + s).astype(BF16)
-            return carry
-
-        def send_opposite():
+    def multiply_one(j, s):
+        own[j, s] = factors(j, x + 1 + s).astype(BF16)
+
+    def send_one(j, s):
+        if s == OPP:
             opposite[j] = [
                 rcopy(own.at[j, OPP, top], fwd.at[j, 0], x_ss.at[j, 0], x_rs.at[j, 0], right),
                 rcopy(own.at[j, OPP, low], fwd.at[j, 1], x_ss.at[j, 1], x_rs.at[j, 1], left),
             ]
             for copy in opposite[j]:
                 copy.start()
-
-        if j == 0:
-            one(OPP, 0)
-            send_opposite()
-            one(R, 0)
-            one(L, 0)
+        elif s == R:
+            send(own.at[j, R, low], got.at[j, 0, low], x_ss.at[j, 2], x_rs.at[j, 2], right)
         else:
-            lax.fori_loop(0, 3, one, 0)
-            send_opposite()
-        send(own.at[j, R, low], got.at[j, 0, low], x_ss.at[j, 2], x_rs.at[j, 2], right)
-        send(own.at[j, L, top], got.at[j, 1, top], x_ss.at[j, 3], x_rs.at[j, 3], left)
+            send(own.at[j, L, top], got.at[j, 1, top], x_ss.at[j, 3], x_rs.at[j, 3], left)
+
+    def multiply(j):
+        def one(s, carry):
+            multiply_one(j, s)
+            return carry
+
+        lax.fori_loop(0, 3, one, 0)
+        for s in (OPP, R, L):
+            send_one(j, s)
 
     def add_on(j):
         for n, (s, part, to) in enumerate(((R, top, right), (L, low, left))):
@@ -354,11 +375,19 @@
             if side in (SAME, HIGH):
                 local.append(stay())
 
-    multiply(0)
-    run(steps_b[1:10])
+    multiply_one(0, OPP)
+    send_one(0, OPP)
+    go(2, "v20", "v21")
+    multiply_one(0, R)
+    send_one(0, R)
+    go(2, "vl0")
+    multiply_one(0, L)
+    send_one(0, L)
+    go(2, "v30", "v31", "vl1", "vl2", "vl3", "take")
     add_on(0)
-    run(steps_b[10:])
-    multiply(1)
+    for s in (OPP, R, L):
+        multiply_one(1, s)
+        send_one(1, s)
 
     loads[4].wait()
     loads[5].wait()
@@ -542,18 +571,40 @@
         copy.wait()
 
 
-def arrange(gate_t, up_t, down, ig_main, ig_tail, grad_gate, grad_up, grad_down, input_grad):
+def arrange(
+    gate_t, up_t, down, ig_main, ig_tail, grad_gate, grad_up, grad_down, input_grad,
+    vg, vu, vd, vt, tg, tu, vi, sem,
+):
     main = ig_main.shape[0]
     rest = input_grad.shape[0] - main
     core = lax.rem(lax.axis_index("tensor"), 2)
-    ends = ig_tail[...].astype(F32)
-    input_grad[0:main, :] = ig_main[...]
-    input_grad[main:, :] = jnp.where(core == 0, ends[0:rest], ends[rest:]).astype(BF16)
-    for n in range(gate_t.shape[0] // 128):
-        at = pl.ds(n * 128, 128)
-        grad_gate[:, at] = gate_t[at, :].T
-        grad_up[:, at] = up_t[at, :].T
-    grad_down[...] = down[...]
+    moves = [
+        pltpu.make_async_copy(src, dst, sem.at[n])
+        for n, (src, dst) in enumerate(
+            ((gate_t, vg), (up_t, vu), (down, vd), (ig_main, vi.at[pl.ds(0, main), :]), (ig_tail, vt))
+        )
+    ]
+    backs = [
+        pltpu.make_async_copy(src, dst, sem.at[5 + n])
+        for n, (src, dst) in enumerate(((tg, grad_gate), (tu, grad_up), (vd, grad_down), (vi, input_grad)))
+    ]
+    for move in moves:
+        move.start()
+    for n, (src, dst) in enumerate(((vg, tg), (vu, tu))):
+        moves[n].wait()
+        for k in range(src.shape[0] // 128):
+            at = pl.ds(k * 128, 128)
+            dst[:, at] = src[at, :].T
+        backs[n].start()
+    moves[2].wait()
+    backs[2].start()
+    moves[3].wait()
+    moves[4].wait()
+    ends = vt[...].astype(F32)
+    vi[main:, :] = jnp.where(core == 0, ends[0:rest], ends[rest:]).astype(BF16)
+    backs[3].start()
+    for back in backs:
+        back.wait()
 
 
 def local(inputs, out_grad, w_gate, w_up, w_down):
@@ -612,8 +663,13 @@
     grad_gate, grad_up, grad_down, input_grad = pl.pallas_call(
         arrange,
         out_shape=(arr(block, units), arr(block, units), arr(units, block), arr(rows, width)),
-        in_specs=[vmem] * 5,
-        out_specs=(vmem,) * 4,
+        in_specs=[any_] * 5,
+        out_specs=(any_,) * 4,
+        scratch_shapes=[
+            pltpu.VMEM((units, block), BF16), pltpu.VMEM((units, block), BF16), pltpu.VMEM((units, block), BF16),
+            pltpu.VMEM((16, width), BF16), pltpu.VMEM((block, units), BF16), pltpu.VMEM((block, units), BF16),
+            pltpu.VMEM((rows, width), BF16), dma((9,)),
+        ],
     )(*outs[:5])
     return (input_grad[None], grad_gate, grad_up, grad_down)
 

time: 186 us -> 176 us (0.946)
  Pallas kernels: 185 us -> 175 us
    pallas_call x1, Pallas kernels: 181 us -> 172 us  [local(): pl.pallas_call(functools.partial(kernel, scale), out_shape=(arr(units, bl...]
where the time goes in v4:
time: 176 us
  Pallas kernels  175 us (99%)
    pallas_call x1, Pallas kernels, local(): pl.pallas_call(functools.partial(kernel, scale), out_shape=(arr(units, bl...  172 us

profile of v4, /device:TPU:64, one launch (start us, length us, event | category | flops | bytes accessed | tf_op | source)
XLA Modules:
  0.0 175.6 jit_solution(3357494224642187288)
XLA Ops:
  0.6 171.6 %shard_map.84 = (bf16[896,512]{1,0:T(8,128)(2,1)}, bf16[896,512]{1,0:T(8,128)(2,1)}, bf16[896,512]{1,0:T(8,128)(2,1)}, bf16[32,4096]{1,0:T(8,128)(2,1)}, bf16[16...) custom-call(bf16[40,4096]{1,0:T(8,128)(2,1)} %bitcast.3, ...), custom_call_target="tpu_custom_call" | custom-call | flops 37580963840 | bytes 22020096 | tf_op jit(solution)/shard_map/pallas_call | solution.py:624
  172.2 3.2 %shard_map.85 = (bf16[512,896]{1,0:T(8,128)(2,1)}, bf16[512,896]{1,0:T(8,128)(2,1)}, bf16[896,512]{1,0:T(8,128)(2,1)}, bf16[40,4096]{1,0:T(8,128)(2,1)}) custom-call(bf16[896,512]{1,0:T(8,128)(2,1)} %get-tuple-element.13.gate_t, bf16[896,512]{1,0:T(8,128)(2,1)} %get-tuple-element.14.up_t, bf16[896,512]{1,0:T(8,128)(2,1)} %get-tuple-element.15.down, ...), custom_call_target="tpu_custom_call" | custom-call | tf_op jit(solution)/shard_map/pallas_call | solution.py:663

commit v5 on v4

--- a/solution.py
+++ b/solution.py
@@ -283,9 +283,7 @@
     go(2, "v00", "v01")
     gate(1)
     go(1, "vl2", "vl3")
-    go(2, "ulast")
     gate(len(gates))
-    go(2, "v10", "v11")
     go(1, "take")
 
     def factors(j, xx):
@@ -377,10 +375,10 @@
 
     multiply_one(0, OPP)
     send_one(0, OPP)
-    go(2, "v20", "v21")
+    go(2, "ulast", "v10", "v11")
     multiply_one(0, R)
     send_one(0, R)
-    go(2, "vl0")
+    go(2, "v20", "v21", "vl0")
     multiply_one(0, L)
     send_one(0, L)
     go(2, "v30", "v31", "vl1", "vl2", "vl3", "take")
@@ -414,8 +412,8 @@
 
     lax.fori_loop(0, pieces, grad_piece, 0)
 
+    multiply(2)
     add_on(1)
-    multiply(2)
     prepare(0)
 
     order = (2, 1, 3, 0)
@@ -510,8 +508,6 @@
     finish(2)
     prepare(3)
     prepare(4)
-    add_on(4)
-    finish(3)
 
     def collect(arrivals, kept, k):
         places = [
@@ -541,6 +537,9 @@
         if r:
             q = 11 + r
             send(sums.at[k], r_hbm.at[q], r_ss.at[q], r_rs.at[q], uv_dev(ring(u, r), v))
+        if k == 1:
+            add_on(4)
+            finish(3)
     prepare(5)
     add_on(5)
     collect([12, 13, 14], None, 4)

time: 176 us -> 173 us (0.983)
  Pallas kernels: 175 us -> 172 us
    pallas_call x1, Pallas kernels: 172 us -> 169 us  [local(): pl.pallas_call(functools.partial(kernel, scale), out_shape=(arr(units, bl...]
where the time goes in v5:
time: 173 us
  Pallas kernels  172 us (99%)
    pallas_call x1, Pallas kernels, local(): pl.pallas_call(functools.partial(kernel, scale), out_shape=(arr(units, bl...  169 us

profile of v5, /device:TPU:64, one launch (start us, length us, event | category | flops | bytes accessed | tf_op | source)
XLA Modules:
  0.0 172.8 jit_solution(4297593160351955022)
XLA Ops:
  0.6 168.8 %shard_map.84 = (bf16[896,512]{1,0:T(8,128)(2,1)}, bf16[896,512]{1,0:T(8,128)(2,1)}, bf16[896,512]{1,0:T(8,128)(2,1)}, bf16[32,4096]{1,0:T(8,128)(2,1)}, bf16[16...) custom-call(bf16[40,4096]{1,0:T(8,128)(2,1)} %bitcast.3, ...), custom_call_target="tpu_custom_call" | custom-call | flops 37580963840 | bytes 22020096 | tf_op jit(solution)/shard_map/pallas_call | solution.py:623
  169.4 3.2 %shard_map.85 = (bf16[512,896]{1,0:T(8,128)(2,1)}, bf16[512,896]{1,0:T(8,128)(2,1)}, bf16[896,512]{1,0:T(8,128)(2,1)}, bf16[40,4096]{1,0:T(8,128)(2,1)}) custom-call(bf16[896,512]{1,0:T(8,128)(2,1)} %get-tuple-element.13.gate_t, bf16[896,512]{1,0:T(8,128)(2,1)} %get-tuple-element.14.up_t, bf16[896,512]{1,0:T(8,128)(2,1)} %get-tuple-element.15.down, ...), custom_call_target="tpu_custom_call" | custom-call | tf_op jit(solution)/shard_map/pallas_call | solution.py:662

commit v6 on v5

--- a/solution.py
+++ b/solution.py
@@ -412,10 +412,6 @@
 
     lax.fori_loop(0, pieces, grad_piece, 0)
 
-    multiply(2)
-    add_on(1)
-    prepare(0)
-
     order = (2, 1, 3, 0)
     strip = 512
     strips = half // strip
@@ -479,14 +475,17 @@
         spread(k)
 
     give_piece(0)
+    multiply(2)
+    add_on(1)
+    prepare(0)
     give_piece(1)
+    p0 = fetch(0)
     finish(0)
-    p0 = fetch(0)
-    give_piece(2)
     sum_piece(0, p0)
     p1 = fetch(1)
+    give_piece(2)
+    send_piece(0)
     multiply(3)
-    send_piece(0)
     sum_piece(1, p1)
     add_on(2)
     give_piece(3)

time: 173 us -> 170 us (0.983)
  Pallas kernels: 172 us -> 168 us
    pallas_call x1, Pallas kernels: 169 us -> 165 us  [local(): pl.pallas_call(functools.partial(kernel, scale), out_shape=(arr(units, bl...]
where the time goes in v6:
time: 170 us; the launch traced here: 169 us
  Pallas kernels  168 us (99%)
    pallas_call x1, Pallas kernels, local(): pl.pallas_call(functools.partial(kernel, scale), out_shape=(arr(units, bl...  165 us

profile of v6, /device:TPU:64, one launch (start us, length us, event | category | flops | bytes accessed | tf_op | source)
XLA Modules:
  0.0 169.1 jit_solution(18244985242853358166)
XLA Ops:
  0.6 165.1 %shard_map.84 = (bf16[896,512]{1,0:T(8,128)(2,1)}, bf16[896,512]{1,0:T(8,128)(2,1)}, bf16[896,512]{1,0:T(8,128)(2,1)}, bf16[32,4096]{1,0:T(8,128)(2,1)}, bf16[16...) custom-call(bf16[40,4096]{1,0:T(8,128)(2,1)} %bitcast.3, ...), custom_call_target="tpu_custom_call" | custom-call | flops 37580963840 | bytes 22020096 | tf_op jit(solution)/shard_map/pallas_call | solution.py:622
  165.7 3.2 %shard_map.85 = (bf16[512,896]{1,0:T(8,128)(2,1)}, bf16[512,896]{1,0:T(8,128)(2,1)}, bf16[896,512]{1,0:T(8,128)(2,1)}, bf16[40,4096]{1,0:T(8,128)(2,1)}) custom-call(bf16[896,512]{1,0:T(8,128)(2,1)} %get-tuple-element.13.gate_t, bf16[896,512]{1,0:T(8,128)(2,1)} %get-tuple-element.14.up_t, bf16[896,512]{1,0:T(8,128)(2,1)} %get-tuple-element.15.down, ...), custom_call_target="tpu_custom_call" | custom-call | tf_op jit(solution)/shard_map/pallas_call | solution.py:661
